TPU v7x, 256 devices: a whole 4x4x8 slice. The times are simulated.
256 devices in a mesh: lat: 16 (over x_hi, y, core), lon: 8 (over z), section: 2 (over x_lo).
Axes of the slice: x: 4 (x_hi: 2, x_lo: 2; x = x_hi * 2 + x_lo), y: 4, z: 8, core: 2. Of those that a mesh axis runs over, the one named last changes fastest.
Arguments:
- fields: bfloat16 [2, 384, 128, 1536], P('section', 'lat', 'lon'), may hold values from -6 to 6, as said below
- land_sea: int32 [384, 128], P('lat', 'lon'), may hold values 0 or 1
- pole_valid: int32 [384, 128], P('lat', 'lon'), may hold values from 0 to 1, as said below
- lead_steps: int32 [2, 2], P('section'), may hold values from 0 to 39
- lead_table: float32 [40, 1536], replicated, may hold values from -3 to 3
- land_vector: float32 [1536], replicated, may hold values from -3 to 3
- norm_gain: float32 [2, 1536], P('section'), may hold values from 0.1 to 1.9
- w_query: bfloat16 [2, 1536, 768], P('section'), may hold values from -0.15309311 to 0.15309311
- w_key: bfloat16 [2, 1536, 768], P('section'), may hold values from -0.20412415 to 0.20412415
- w_value: bfloat16 [2, 1536, 768], P('section'), may hold values from -0.15625 to 0.15625
- w_out: bfloat16 [2, 768, 1536], P('section'), may hold values from -0.21875 to 0.21875
- logit_scale: float32 [2, 12], P('section'), may hold values from 2 to 400
Outputs:
- rollout: bfloat16 [2, 384, 128, 1536], P('section', 'lat', 'lon')
Inputs may be any that keep to these rules, and one draw needn't show every extreme that they name: `fields`: each initial time's state; entries of order one. `pole_valid`: in each longitude column, 0 on its own number of first latitude rows and its own number of last latitude rows, each number 1 to 6, and 1 elsewhere; some column has 6 on both sides.
All inputs are finite; a program needn't handle non-finite values. No bound on the sum of `land_sea` on one device may be relied on, other than what follows from the above.
Results may differ from a plain program's by a relative error of at most 0.007.
Values may be sent and summed in bfloat16 or wider, within the bound.
A program may use at most 128 MiB of HBM per device.

v0:
```python
import functools

import jax
import jax.numpy as jnp
from jax import lax
from jax.experimental import pallas as pl
from jax.experimental.pallas import tpu as pltpu
from jax.sharding import PartitionSpec as P

R = 6
ROWS = 24
COLS = 16
CELLS = ROWS * COLS
D = 1536
INNER = 768
HEADS = 12
HEAD = 64
LANES = 256
GROUPS = INNER // LANES
PER_GROUP = LANES // HEAD
PROWS = 8
PCELLS = PROWS * COLS
PIECES = ROWS // PROWS
BROWS = 4
BCELLS = BROWS * COLS
BLOCKS = ROWS // BROWS
STRIP = PROWS * R
OWN = (ROWS + 2 * R) * COLS
SIDE = (ROWS + 2 * PROWS) * R
REACH = 112
SPARE = 32
WIDE = 128
LOG2E = 1.4426950408889634
LOW = -1e30
F32 = jnp.float32
BF16 = jnp.bfloat16

Z_LEFT = 0
Z_RIGHT = PIECES
EDGE = 2 * PIECES
SLOTS = EDGE + 6


def dot_t(a, b):
    return lax.dot_general(a, b, (((1,), (1,)), ((), ())), preferred_element_type=F32)


def dot(a, b):
    return jnp.dot(a, b, preferred_element_type=F32)


def iota(shape, dim):
    return lax.broadcasted_iota(jnp.int32, shape, dim)


def cell_column(grid, row, col, cells):
    picks = (iota((cells, grid.shape[0]), 1) == row).astype(F32).astype(BF16)
    rows = dot(picks, grid.astype(BF16))
    hit = iota(rows.shape, 1) == col
    return jnp.sum(jnp.where(hit, rows, 0.0), axis=1, keepdims=True)


def key_flags(row, col, valid, cells):
    lane = iota((cells, WIDE), 1)
    hit = (lane == row) | (lane == col + 48)
    flags = jnp.where(lane == 100, valid, jnp.where(hit, 1.0, 0.0))
    return flags.astype(BF16)


def kernel(
    lat_count,
    lon_count,
    lead_steps,
    logit_scale,
    fields,
    land_sea,
    pole_valid,
    lead_table,
    land_vector,
    norm_gain,
    w_query,
    w_key,
    w_value,
    w_out,
    out,
    x_buf,
    state,
    wq,
    wk,
    wv,
    wo,
    query,
    own,
    left,
    right,
    strips,
    flag_own,
    flag_left,
    flag_right,
    land,
    attended,
    ones_block,
    pole_mine,
    pole_side,
    load_sem,
    out_sem,
    send_sem,
    recv_sem,
    sec_send,
    sec_recv,
    pole_send,
    pole_recv,
):
    lat = lax.axis_index("lat")
    lon = lax.axis_index("lon")
    sec = lax.axis_index("section")
    west = lax.rem(lon + lon_count - 1, lon_count)
    east = lax.rem(lon + 1, lon_count)
    other = 1 - sec
    flip = lax.rem(lat, 2)
    has_up = lat > 0
    has_down = lat < lat_count - 1
    early = lat - 1 + 2 * flip
    late = lat + 1 - 2 * flip
    has_early = jnp.where(flip == 0, has_up, has_down)
    has_late = jnp.where(flip == 0, has_down, has_up)

    loads = [
        pltpu.make_async_copy(src, dst, load_sem.at[i])
        for i, (src, dst) in enumerate(
            (
                (fields, x_buf.at[0]),
                (w_query, wq),
                (w_key, wk),
                (w_value, wv),
                (w_out, wo),
            )
        )
    ]
    for load in loads:
        load.start()

    for buf in (left, right):
        for l in (0, 1):
            buf[l, pl.ds(0, STRIP), :] = jnp.zeros((STRIP, D), BF16)
            buf[l, pl.ds(192, SIDE - 192), :] = jnp.zeros((SIDE - 192, D), BF16)
    for l in (0, 1):
        own[l, pl.ds(0, R * COLS), :] = jnp.zeros((R * COLS, D), BF16)
        own[l, pl.ds(OWN - R * COLS, R * COLS), :] = jnp.zeros((R * COLS, D), BF16)
    pole_mine[...] = jnp.zeros((ROWS, 128), F32)
    pole_mine[:, pl.ds(0, COLS)] = pole_valid[...].astype(F32)

    barrier = pltpu.get_barrier_semaphore()
    pl.semaphore_signal(barrier, inc=1, device_id={"lon": west})
    pl.semaphore_signal(barrier, inc=1, device_id={"lon": east})
    pl.semaphore_signal(barrier, inc=1, device_id={"section": other})

    @pl.when(has_early)
    def _():
        pl.semaphore_signal(barrier, inc=1, device_id={"lat": early})

    @pl.when(has_late)
    def _():
        pl.semaphore_signal(barrier, inc=1, device_id={"lat": late})

    pl.semaphore_wait(barrier, 3 + has_early.astype(jnp.int32) + has_late.astype(jnp.int32))

    def remote(src, dst, send, recv, device):
        return pltpu.make_async_remote_copy(
            src_ref=src, dst_ref=dst, send_sem=send, recv_sem=recv, device_id=device
        )

    def piece_at(p):
        return p + flip * (PIECES - 1 - 2 * p)

    def block_at(i):
        return i + flip * (BLOCKS - 1 - 2 * i)

    pole_copies = (
        remote(pole_mine, pole_side.at[1], pole_send.at[0], pole_recv.at[0], {"lon": west}),
        remote(pole_mine, pole_side.at[0], pole_send.at[1], pole_recv.at[1], {"lon": east}),
    )
    for copy in pole_copies:
        copy.start()

    def z_copies(l, p):
        c = piece_at(p)
        src = pl.ds(pl.multiple_of(c * STRIP, 16), STRIP)
        dst = pl.ds(pl.multiple_of((c + 1) * STRIP, 16), STRIP)
        return (
            remote(
                strips.at[l, 0, src],
                right.at[l, dst],
                send_sem.at[l, Z_LEFT + p],
                recv_sem.at[l, Z_LEFT + p],
                {"lon": west},
            ),
            remote(
                strips.at[l, 1, src],
                left.at[l, dst],
                send_sem.at[l, Z_RIGHT + p],
                recv_sem.at[l, Z_RIGHT + p],
                {"lon": east},
            ),
        )

    def edge_copies(l, which, parts):
        upper = flip if which else 1 - flip
        device = {"lat": late if which else early}
        base = EDGE + 3 * which
        o_src = pl.multiple_of((1 - upper) * (CELLS - R * COLS) + R * COLS, 16)
        o_dst = pl.multiple_of(upper * (OWN - R * COLS), 16)
        s_src = pl.multiple_of(STRIP + (1 - upper) * (PIECES - 1) * STRIP, 16)
        s_dst = pl.multiple_of(upper * (PIECES + 1) * STRIP, 16)
        copies = []
        for j in parts:
            buf = (own, left, right)[j]
            src, dst, size = (o_src, o_dst, R * COLS) if j == 0 else (s_src, s_dst, STRIP)
            copies.append(
                remote(
                    buf.at[l, pl.ds(src, size)],
                    buf.at[l, pl.ds(dst, size)],
                    send_sem.at[l, base + j],
                    recv_sem.at[l, base + j],
                    device,
                )
            )
        return copies

    def edge_when(which, act):
        pl.when(has_late if which else has_early)(act)

    def start_edge_own(l, which):
        def act():
            edge_copies(l, which, (0,))[0].start()

        edge_when(which, act)

    def start_edge_sides(l, which):
        def act():
            for copy in edge_copies(l, which, (1, 2)):
                copy.start()

        edge_when(which, act)

    def wait_edges(l, which):
        upper = flip if which else 1 - flip
        base = EDGE + 3 * which
        o_dst = pl.multiple_of((1 - upper) * (OWN - R * COLS), 16)
        s_dst = pl.multiple_of((1 - upper) * (PIECES + 1) * STRIP, 16)

        def act():
            device = {"lat": late if which else early}
            for j, (buf, start, size) in enumerate(
                ((own, o_dst, R * COLS), (left, s_dst, STRIP), (right, s_dst, STRIP))
            ):
                ref = buf.at[l, pl.ds(start, size)]
                remote(
                    ref, ref, send_sem.at[l, base + j], recv_sem.at[l, base + j], device
                ).wait_recv()

        edge_when(which, act)

    def wait_z(l, p):
        for copy in z_copies(l, p):
            copy.wait_recv()

    def section_copy(i):
        rows = pl.ds(pl.multiple_of(block_at(i) * BCELLS, BCELLS), BCELLS)
        return remote(
            state.at[rows], x_buf.at[1, rows], sec_send.at[i], sec_recv.at[i], {"section": other}
        )

    def out_copy(i):
        rows = pl.ds(pl.multiple_of(block_at(i) * BCELLS, BCELLS), BCELLS)
        return pltpu.make_async_copy(state.at[rows], out.at[rows], out_sem.at[i])

    cell = iota((CELLS, 1), 0)
    land[...] = cell_column(
        land_sea[...].astype(F32), lax.shift_right_logical(cell, 4), cell & 15, CELLS
    )
    same = lax.shift_right_logical(iota((LANES, LANES), 0), 6) == lax.shift_right_logical(
        iota((LANES, LANES), 1), 6
    )
    ones_block[...] = jnp.where(same, 1.0, 0.0).astype(BF16)

    up_flag = has_up.astype(F32)
    down_flag = has_down.astype(F32)

    def build_flags():
        cell = iota((OWN, 1), 0)
        row = lax.shift_right_logical(cell, 4)
        col = cell & 15
        inside = cell_column(pole_mine[...], row - R, col, OWN)
        valid = jnp.where(row < R, up_flag, jnp.where(row >= R + ROWS, down_flag, inside))
        flag_own[...] = key_flags(row, col + R, valid, OWN)
        cell = iota((SIDE, 1), 0)
        row = jnp.floor((cell.astype(F32) + 0.5) * (1.0 / R)).astype(jnp.int32)
        col = cell - R * row
        row = row - (PROWS - R)
        for s, ref in ((0, flag_left), (1, flag_right)):
            picked = col + (COLS - R if s == 0 else 0)
            inside = cell_column(pole_side[s], row - R, picked, SIDE)
            valid = jnp.where(row < R, up_flag, jnp.where(row >= R + ROWS, down_flag, inside))
            ref[...] = key_flags(row, col + (0 if s == 0 else R + COLS), valid, SIDE)

    def unit(x):
        parts = []
        for t in range(GROUPS):
            part = x[:, t * LANES : (t + 1) * LANES]
            square = part * part
            high = square.astype(BF16)
            low = (square - high.astype(F32)).astype(BF16)
            total = dot(high, ones_block[...]) + dot(low, ones_block[...])
            parts.append((part * lax.rsqrt(total * (1.0 / HEAD) + 1e-06)).astype(BF16))
        return jnp.concatenate(parts, axis=1)

    pick_row = iota((2 * STRIP, PCELLS), 0)
    pick_cell = iota((2 * STRIP, PCELLS), 1)
    pick_side = (pick_row >= STRIP).astype(jnp.int32)
    pick_row = pick_row - STRIP * pick_side
    pick_line = jnp.floor((pick_row.astype(F32) + 0.5) * (1.0 / R)).astype(jnp.int32)
    target = pick_line * COLS + (pick_row - R * pick_line) + (COLS - R) * pick_side
    pick = jnp.where(pick_cell == target, 1.0, 0.0).astype(BF16)

    lead_index = iota((lead_table.shape[0], 1), 0)
    lead_rows = [
        jnp.sum(
            jnp.where(lead_index == lead_steps[0, l], lead_table[...], 0.0), axis=0, keepdims=True
        )
        for l in (0, 1)
    ]

    def project(l, p):
        c = piece_at(p)
        rows = pl.ds(pl.multiple_of(c * PCELLS, PCELLS), PCELLS)
        cond = (
            x_buf[l, rows, :].astype(F32) + lead_rows[l] + land[rows, :] * land_vector[...]
        )
        mean_square = jnp.mean(cond * cond, axis=1, keepdims=True)
        normed = (cond * lax.rsqrt(mean_square + 1e-05) * norm_gain[...]).astype(BF16)
        inner_rows = pl.ds(pl.multiple_of(c * PCELLS + R * COLS, 16), PCELLS)
        strip_rows = pl.ds(pl.multiple_of(c * STRIP, 16), STRIP)

        def finish(part, lanes):
            own[l, inner_rows, lanes] = part
            sent = dot(pick, part).astype(BF16)
            strips[l, 0, strip_rows, lanes] = sent[:STRIP]
            strips[l, 1, strip_rows, lanes] = sent[STRIP:]

        finish(unit(dot(normed, wk[...])), pl.ds(0, INNER))
        finish(dot(normed, wv[...]).astype(BF16), pl.ds(INNER, INNER))
        for copy in z_copies(l, p):
            copy.start()
        query[rows, :] = unit(dot(normed, wq[...]))

    def attend(l, i):
        b = block_at(i)
        rows = pl.ds(pl.multiple_of(b * BCELLS, BCELLS), BCELLS)
        own_rows = pl.ds(pl.multiple_of(b * BCELLS, BCELLS), 16 * COLS)
        side_rows = pl.ds(
            pl.multiple_of(16 * lax.shift_right_logical(6 * b + 3, 2), 16), REACH
        )
        spare = jnp.zeros((SPARE, LANES), BF16)
        q_cell = iota((BCELLS, WIDE), 0)
        lane = iota((BCELLS, WIDE), 1)
        q_row = lax.shift_right_logical(q_cell, 4) + b * BROWS
        q_col = q_cell & 15
        near_row = (lane >= q_row) & (lane <= q_row + 2 * R)
        near_col = (lane - 48 >= q_col) & (lane - 48 <= q_col + 2 * R)
        wanted = jnp.where(near_row | near_col | (lane == 100), 1.0, 0.0).astype(BF16)
        flags = jnp.concatenate(
            [flag_own[own_rows, :], flag_left[side_rows, :], flag_right[side_rows, :], spare[:, :WIDE]], axis=0
        )
        bias = jnp.where(dot_t(wanted, flags) > 2.5, 0.0, LOW)
        lane_head = lax.shift_right_logical(iota((1, LANES), 1), 6)
        for g in range(GROUPS):
            k_lanes = pl.ds(g * LANES, LANES)
            v_lanes = pl.ds(INNER + g * LANES, LANES)
            q = query[rows, k_lanes]
            q_all = jnp.concatenate(
                [
                    jnp.where(lane_head == h, q, jnp.zeros_like(q))
                    for h in range(PER_GROUP)
                ],
                axis=0,
            )
            keys = jnp.concatenate(
                [
                    own[l, own_rows, k_lanes],
                    left[l, side_rows, k_lanes],
                    right[l, side_rows, k_lanes],
                    spare,
                ],
                axis=0,
            )
            values = jnp.concatenate(
                [
                    own[l, own_rows, v_lanes],
                    left[l, side_rows, v_lanes],
                    right[l, side_rows, v_lanes],
                    spare,
                ],
                axis=0,
            )
            scores = dot_t(q_all, keys)
            probs = []
            inverses = []
            for h in range(PER_GROUP):
                factor = logit_scale[0, g * PER_GROUP + h] * (LOG2E / HEAD)
                part = scores[h * BCELLS : (h + 1) * BCELLS] * factor + bias
                prob = jnp.exp2(part - jnp.max(part, axis=1, keepdims=True))
                inverses.append(1.0 / jnp.sum(prob, axis=1, keepdims=True))
                probs.append(prob.astype(BF16))
            mixed = dot(jnp.concatenate(probs, axis=0), values)
            total = jnp.zeros((BCELLS, LANES), F32)
            for h in range(PER_GROUP):
                part = mixed[h * BCELLS : (h + 1) * BCELLS] * inverses[h]
                total = jnp.where(lane_head == h, part, total)
            attended[:, k_lanes] = total.astype(BF16)
        moved = x_buf[l, rows, :].astype(F32) + dot(attended[...], wo[...])
        state[rows, :] = moved.astype(BF16)

    def project_loop(l, low, high):
        def body(p, carry):
            project(l, p)
            return carry

        lax.fori_loop(low, high, body, 0)

    for load in loads[:4]:
        load.wait()
    project_loop(0, 0, 1)
    start_edge_own(0, 0)
    project_loop(0, 1, PIECES)
    start_edge_own(0, 1)
    loads[4].wait()
    for copy in pole_copies:
        copy.wait_recv()
    build_flags()
    wait_z(0, 0)
    start_edge_sides(0, 0)
    wait_z(0, 1)
    wait_edges(0, 0)

    def first_body(i, carry):
        @pl.when(i == 2)
        def _():
            wait_z(0, 2)
            start_edge_sides(0, 1)

        @pl.when(i == 4)
        def _():
            wait_edges(0, 1)

        attend(0, i)
        section_copy(i).start()
        return carry

    lax.fori_loop(0, BLOCKS, first_body, 0)

    for i in (0, 1):
        section_copy(i).wait_recv()
    project_loop(1, 0, 1)
    start_edge_own(1, 0)
    for i in (2, 3):
        section_copy(i).wait_recv()
    project_loop(1, 1, 2)
    for i in range(BLOCKS):
        section_copy(i).wait_send()
    wait_z(1, 0)
    start_edge_sides(1, 0)
    wait_z(1, 1)
    wait_edges(1, 0)

    def second_body(i, carry):
        @pl.when(i == 2)
        def _():
            for j in (4, 5):
                section_copy(j).wait_recv()
            project(1, 2)
            start_edge_own(1, 1)
            wait_z(1, 2)
            start_edge_sides(1, 1)

        @pl.when(i == 4)
        def _():
            wait_edges(1, 1)

        attend(1, i)
        out_copy(i).start()
        return carry

    lax.fori_loop(0, BLOCKS, second_body, 0)

    for i in range(BLOCKS):
        out_copy(i).wait()
    for copy in pole_copies:
        copy.wait_send()
    for l in (0, 1):
        for p in range(PIECES):
            for copy in z_copies(l, p):
                copy.wait_send()
        for which in (0, 1):

            def act(l=l, which=which):
                for copy in edge_copies(l, which, (0, 1, 2)):
                    copy.wait_send()

            edge_when(which, act)


def per_device(
    lat_count,
    lon_count,
    fields,
    land_sea,
    pole_valid,
    lead_steps,
    lead_table,
    land_vector,
    norm_gain,
    w_query,
    w_key,
    w_value,
    w_out,
    logit_scale,
):
    vmem = pl.BlockSpec(memory_space=pltpu.VMEM)
    smem = pl.BlockSpec(memory_space=pltpu.SMEM)
    hbm = pl.BlockSpec(memory_space=pl.ANY)
    result = pl.pallas_call(
        functools.partial(kernel, lat_count, lon_count),
        out_shape=jax.ShapeDtypeStruct((CELLS, D), BF16),
        in_specs=[smem, smem, hbm, vmem, vmem, vmem, vmem, vmem, hbm, hbm, hbm, hbm],
        out_specs=hbm,
        scratch_shapes=[
            pltpu.VMEM((2, CELLS, D), BF16),
            pltpu.VMEM((CELLS, D), BF16),
            pltpu.VMEM((D, INNER), BF16),
            pltpu.VMEM((D, INNER), BF16),
            pltpu.VMEM((D, INNER), BF16),
            pltpu.VMEM((INNER, D), BF16),
            pltpu.VMEM((CELLS, INNER), BF16),
            pltpu.VMEM((2, OWN, D), BF16),
            pltpu.VMEM((2, SIDE, D), BF16),
            pltpu.VMEM((2, SIDE, D), BF16),
            pltpu.VMEM((2, 2, PIECES * STRIP, D), BF16),
            pltpu.VMEM((OWN, WIDE), BF16),
            pltpu.VMEM((SIDE, WIDE), BF16),
            pltpu.VMEM((SIDE, WIDE), BF16),
            pltpu.VMEM((CELLS, 1), F32),
            pltpu.VMEM((BCELLS, INNER), BF16),
            pltpu.VMEM((LANES, LANES), BF16),
            pltpu.VMEM((ROWS, 128), F32),
            pltpu.VMEM((2, ROWS, 128), F32),
            pltpu.SemaphoreType.DMA((5,)),
            pltpu.SemaphoreType.DMA((BLOCKS,)),
            pltpu.SemaphoreType.DMA((2, SLOTS)),
            pltpu.SemaphoreType.DMA((2, SLOTS)),
            pltpu.SemaphoreType.DMA((BLOCKS,)),
            pltpu.SemaphoreType.DMA((BLOCKS,)),
            pltpu.SemaphoreType.DMA((2,)),
            pltpu.SemaphoreType.DMA((2,)),
        ],
        compiler_params=pltpu.CompilerParams(
            collective_id=0, has_side_effects=True, vmem_limit_bytes=56 * 1024 * 1024
        ),
    )(
        lead_steps,
        logit_scale,
        fields.reshape(CELLS, D),
        land_sea,
        pole_valid,
        lead_table,
        land_vector.reshape(1, D),
        norm_gain,
        w_query[0],
        w_key[0],
        w_value[0],
        w_out[0],
    )
    return result.reshape(1, ROWS, COLS, D)


def solution(mesh):
    return jax.shard_map(
        functools.partial(per_device, mesh.shape["lat"], mesh.shape["lon"]),
        mesh=mesh,
        in_specs=(
            P("section", "lat", "lon", None),
            P("lat", "lon"),
            P("lat", "lon"),
            P("section", None),
            P(),
            P(),
            P("section", None),
            P("section", None, None),
            P("section", None, None),
            P("section", None, None),
            P("section", None, None),
            P("section", None),
        ),
        out_specs=P("section", "lat", "lon", None),
        check_vma=False,
    )
```

profile of v0, /device:TPU:6, one launch (start us, length us, event | category | flops | bytes accessed | tf_op | source)
XLA Modules:
  0.0 83.0 jit_solution(2954880519525785880)
XLA Ops:
  0.0 1.3 %reshape.10.land_vector = f32[1,1536]{1,0:T(1,128)} reshape(f32[1536]{0:T(1024)} %param.17) | data formatting | bytes 12288 | tf_op jit(solution)/shard_map/reshape | solution.py:576
  1.3 1.4 %copy.13.land_sea = s32[24,16]{1,0:T(8,128)} copy(s32[24,16]{0,1:T(8,128)} %param.13) | data formatting | bytes 3072 | tf_op args[1]
  2.7 1.4 %copy.14.pole_valid = s32[24,16]{1,0:T(8,128)} copy(s32[24,16]{0,1:T(8,128)} %param.14) | data formatting | bytes 3072 | tf_op args[2]
  4.0 76.6 %shard_map.118 = bf16[384,1536]{1,0:T(8,128)(2,1)} custom-call(s32[1,2]{1,0:T(1,128)} %lead_steps.1, f32[1,12]{1,0:T(1,128)} %logit_scale.1, bf16[384,1536]{1,0:T(8,128)(2,1)} %bitcast.11, s32[24,16]{1,0:T(8,128)} %copy.13.land_sea, s32[24,16]{1,0:T(8,128)} %copy.14.pole_valid, f32[40,1536]{1,0:T(8,128)} %lead_table.1, f32[1,1536]{1,0:T(1,128)} %reshape.10.land_vector, ...), custom_call_target="tpu_custom_call" | custom-call | tf_op jit(solution)/shard_map/pallas_call | solution.py:532
  80.7 2.4 %copy.16 = bf16[1,24,16,1536]{3,2,1,0:T(8,128)(2,1)} copy(bf16[1,24,16,1536]{3,2,1,0:T(8,128)(2,1)} %bitcast.6) | data formatting | bytes 2359296
where the time goes:
time: 83.3 us; the launch traced here: 83 us
  Pallas kernels  76.6 us (92%)
  local copies, waits for them, and re-layouts  6.38 us (8%)
    pallas_call x1, Pallas kernels, per_device(): pl.pallas_call(functools.partial(kernel, lat_count, lon_count), out_shape...  76.6 us
    unnamed x3, local copies, waits for them, and re-layouts  5.09 us

commit v1 on v0

--- a/solution.py
+++ b/solution.py
@@ -35,9 +35,8 @@
 F32 = jnp.float32
 BF16 = jnp.bfloat16
 
-Z_LEFT = 0
-Z_RIGHT = PIECES
-EDGE = 2 * PIECES
+PARTS = PIECES + 2
+EDGE = 2 * PARTS
 SLOTS = EDGE + 6
 
 
@@ -54,10 +53,10 @@
 
 
 def cell_column(grid, row, col, cells):
-    picks = (iota((cells, grid.shape[0]), 1) == row).astype(F32).astype(BF16)
-    rows = dot(picks, grid.astype(BF16))
-    hit = iota(rows.shape, 1) == col
-    return jnp.sum(jnp.where(hit, rows, 0.0), axis=1, keepdims=True)
+    picks = (iota((cells, grid.shape[0]), 1) == col).astype(F32).astype(BF16)
+    found = dot(picks, grid.astype(BF16))
+    hit = iota(found.shape, 1) == row
+    return jnp.sum(jnp.where(hit, found, 0.0), axis=1, keepdims=True)
 
 
 def key_flags(row, col, valid, cells):
@@ -73,18 +72,25 @@
     lead_steps,
     logit_scale,
     fields,
+    land_sea_in,
+    pole_valid_in,
+    lead_table_in,
+    land_vector_in,
+    norm_gain_in,
+    w_query,
+    w_key,
+    w_value,
+    w_out,
+    out,
     land_sea,
     pole_valid,
     lead_table,
     land_vector,
     norm_gain,
-    w_query,
-    w_key,
-    w_value,
-    w_out,
-    out,
     x_buf,
     state,
+    final,
+    normed,
     wq,
     wk,
     wv,
@@ -102,6 +108,8 @@
     ones_block,
     pole_mine,
     pole_side,
+    corners,
+    small_sem,
     load_sem,
     out_sem,
     send_sem,
@@ -125,31 +133,6 @@
     has_early = jnp.where(flip == 0, has_up, has_down)
     has_late = jnp.where(flip == 0, has_down, has_up)
 
-    loads = [
-        pltpu.make_async_copy(src, dst, load_sem.at[i])
-        for i, (src, dst) in enumerate(
-            (
-                (fields, x_buf.at[0]),
-                (w_query, wq),
-                (w_key, wk),
-                (w_value, wv),
-                (w_out, wo),
-            )
-        )
-    ]
-    for load in loads:
-        load.start()
-
-    for buf in (left, right):
-        for l in (0, 1):
-            buf[l, pl.ds(0, STRIP), :] = jnp.zeros((STRIP, D), BF16)
-            buf[l, pl.ds(192, SIDE - 192), :] = jnp.zeros((SIDE - 192, D), BF16)
-    for l in (0, 1):
-        own[l, pl.ds(0, R * COLS), :] = jnp.zeros((R * COLS, D), BF16)
-        own[l, pl.ds(OWN - R * COLS, R * COLS), :] = jnp.zeros((R * COLS, D), BF16)
-    pole_mine[...] = jnp.zeros((ROWS, 128), F32)
-    pole_mine[:, pl.ds(0, COLS)] = pole_valid[...].astype(F32)
-
     barrier = pltpu.get_barrier_semaphore()
     pl.semaphore_signal(barrier, inc=1, device_id={"lon": west})
     pl.semaphore_signal(barrier, inc=1, device_id={"lon": east})
@@ -163,46 +146,96 @@
     def _():
         pl.semaphore_signal(barrier, inc=1, device_id={"lat": late})
 
-    pl.semaphore_wait(barrier, 3 + has_early.astype(jnp.int32) + has_late.astype(jnp.int32))
+    def piece_at(p):
+        return p + flip * (PIECES - 1 - 2 * p)
+
+    def block_at(i):
+        return i + flip * (BLOCKS - 1 - 2 * i)
+
+    def load_piece(p):
+        rows = pl.ds(pl.multiple_of(piece_at(p) * PCELLS, PCELLS), PCELLS)
+        return pltpu.make_async_copy(fields.at[rows], x_buf.at[0, rows], load_sem.at[p])
+
+    load_key = pltpu.make_async_copy(w_key, wk, load_sem.at[PIECES])
+    load_value = pltpu.make_async_copy(w_value, wv, load_sem.at[PIECES + 1])
+    load_query = pltpu.make_async_copy(w_query, wq, load_sem.at[PIECES + 2])
+    load_out = pltpu.make_async_copy(w_out, wo, load_sem.at[PIECES + 3])
+    load_piece(0).start()
+    smalls = [
+        pltpu.make_async_copy(src, dst, small_sem.at[i])
+        for i, (src, dst) in enumerate(
+            (
+                (lead_table_in, lead_table),
+                (land_vector_in, land_vector),
+                (norm_gain_in, norm_gain),
+                (land_sea_in, land_sea),
+                (pole_valid_in, pole_valid),
+            )
+        )
+    ]
+    for small in smalls:
+        small.start()
+    load_key.start()
+    load_value.start()
+    for p in range(1, PIECES):
+        load_piece(p).start()
+
+    def clear_rows(missing, own_start, side_start):
+        @pl.when(missing)
+        def _():
+            for l in (0, 1):
+                own[l, pl.ds(own_start, R * COLS), :] = jnp.zeros((R * COLS, D), BF16)
+                for buf in (left, right):
+                    buf[l, pl.ds(side_start, STRIP), :] = jnp.zeros((STRIP, D), BF16)
+
+    clear_rows(jnp.logical_not(has_up), 0, 0)
+    clear_rows(jnp.logical_not(has_down), OWN - R * COLS, SIDE - STRIP)
+    for small in smalls:
+        small.wait()
+    pole_mine[...] = jnp.zeros((COLS, 128), F32)
+    pole_mine[:, pl.ds(0, ROWS)] = pole_valid[...].astype(F32)
 
     def remote(src, dst, send, recv, device):
         return pltpu.make_async_remote_copy(
             src_ref=src, dst_ref=dst, send_sem=send, recv_sem=recv, device_id=device
         )
 
-    def piece_at(p):
-        return p + flip * (PIECES - 1 - 2 * p)
-
-    def block_at(i):
-        return i + flip * (BLOCKS - 1 - 2 * i)
-
     pole_copies = (
         remote(pole_mine, pole_side.at[1], pole_send.at[0], pole_recv.at[0], {"lon": west}),
         remote(pole_mine, pole_side.at[0], pole_send.at[1], pole_recv.at[1], {"lon": east}),
     )
-    for copy in pole_copies:
-        copy.start()
+    def part_at(p):
+        if isinstance(p, int) and p >= PIECES:
+            base = piece_at(PIECES - 1) * STRIP
+            if p == PIECES:
+                return base + flip * 32, 16
+            return base + (1 - flip) * 16, 32
+        return piece_at(p) * STRIP, STRIP
 
     def z_copies(l, p):
-        c = piece_at(p)
-        src = pl.ds(pl.multiple_of(c * STRIP, 16), STRIP)
-        dst = pl.ds(pl.multiple_of((c + 1) * STRIP, 16), STRIP)
+        start, size = part_at(p)
+        src = pl.ds(pl.multiple_of(start, 16), size)
+        dst = pl.ds(pl.multiple_of(start + STRIP, 16), size)
         return (
             remote(
                 strips.at[l, 0, src],
                 right.at[l, dst],
-                send_sem.at[l, Z_LEFT + p],
-                recv_sem.at[l, Z_LEFT + p],
+                send_sem.at[l, p],
+                recv_sem.at[l, p],
                 {"lon": west},
             ),
             remote(
                 strips.at[l, 1, src],
                 left.at[l, dst],
-                send_sem.at[l, Z_RIGHT + p],
-                recv_sem.at[l, Z_RIGHT + p],
+                send_sem.at[l, PARTS + p],
+                recv_sem.at[l, PARTS + p],
                 {"lon": east},
             ),
         )
+
+    def start_z(l, p):
+        for copy in z_copies(l, p):
+            copy.start()
 
     def edge_copies(l, which, parts):
         upper = flip if which else 1 - flip
@@ -236,30 +269,75 @@
 
         edge_when(which, act)
 
-    def start_edge_sides(l, which):
+    def start_late_sides(l):
         def act():
-            for copy in edge_copies(l, which, (1, 2)):
+            for copy in edge_copies(l, 1, (1, 2)):
                 copy.start()
 
-        edge_when(which, act)
-
-    def wait_edges(l, which):
-        upper = flip if which else 1 - flip
-        base = EDGE + 3 * which
-        o_dst = pl.multiple_of((1 - upper) * (OWN - R * COLS), 16)
-        s_dst = pl.multiple_of((1 - upper) * (PIECES + 1) * STRIP, 16)
-
+        edge_when(1, act)
+
+    def corner_copies(l):
+        rows = pl.ds(pl.multiple_of(flip * (SIDE - STRIP), 16), STRIP)
+        return (
+            remote(
+                corners.at[l, 0],
+                right.at[l, rows],
+                send_sem.at[l, EDGE + 1],
+                recv_sem.at[l, EDGE + 1],
+                {"lon": west},
+            ),
+            remote(
+                corners.at[l, 1],
+                left.at[l, rows],
+                send_sem.at[l, EDGE + 2],
+                recv_sem.at[l, EDGE + 2],
+                {"lon": east},
+            ),
+        )
+
+    def start_corners(l):
         def act():
-            device = {"lat": late if which else early}
+            start = flip * (OWN - R * COLS)
+            rows = pl.ds(pl.multiple_of(start, 16), R * COLS)
+            ref = own.at[l, rows]
+            remote(
+                ref, ref, send_sem.at[l, EDGE], recv_sem.at[l, EDGE], {"lat": early}
+            ).wait_recv()
+            picked = picker(0, STRIP, R * COLS, (1 - flip) * (PROWS - R) * COLS)
+            for lanes in (pl.ds(0, INNER), pl.ds(INNER, INNER)):
+                sent = dot(picked, own[l, rows, lanes]).astype(BF16)
+                corners[l, 0, :, lanes] = sent[:STRIP]
+                corners[l, 1, :, lanes] = sent[STRIP:]
+            for copy in corner_copies(l):
+                copy.start()
+
+        edge_when(0, act)
+
+    def wait_corners(l):
+        def act():
+            for copy in corner_copies(l):
+                copy.wait_recv()
+
+        edge_when(0, act)
+
+    def wait_late(l):
+        o_dst = pl.multiple_of((1 - flip) * (OWN - R * COLS), 16)
+        s_dst = pl.multiple_of((1 - flip) * (SIDE - STRIP), 16)
+
+        def act():
             for j, (buf, start, size) in enumerate(
                 ((own, o_dst, R * COLS), (left, s_dst, STRIP), (right, s_dst, STRIP))
             ):
                 ref = buf.at[l, pl.ds(start, size)]
                 remote(
-                    ref, ref, send_sem.at[l, base + j], recv_sem.at[l, base + j], device
+                    ref,
+                    ref,
+                    send_sem.at[l, EDGE + 3 + j],
+                    recv_sem.at[l, EDGE + 3 + j],
+                    {"lat": late},
                 ).wait_recv()
 
-        edge_when(which, act)
+        edge_when(1, act)
 
     def wait_z(l, p):
         for copy in z_copies(l, p):
@@ -273,7 +351,7 @@
 
     def out_copy(i):
         rows = pl.ds(pl.multiple_of(block_at(i) * BCELLS, BCELLS), BCELLS)
-        return pltpu.make_async_copy(state.at[rows], out.at[rows], out_sem.at[i])
+        return pltpu.make_async_copy(final.at[rows], out.at[rows], out_sem.at[i])
 
     cell = iota((CELLS, 1), 0)
     land[...] = cell_column(
@@ -315,14 +393,17 @@
             parts.append((part * lax.rsqrt(total * (1.0 / HEAD) + 1e-06)).astype(BF16))
         return jnp.concatenate(parts, axis=1)
 
-    pick_row = iota((2 * STRIP, PCELLS), 0)
-    pick_cell = iota((2 * STRIP, PCELLS), 1)
-    pick_side = (pick_row >= STRIP).astype(jnp.int32)
-    pick_row = pick_row - STRIP * pick_side
-    pick_line = jnp.floor((pick_row.astype(F32) + 0.5) * (1.0 / R)).astype(jnp.int32)
-    target = pick_line * COLS + (pick_row - R * pick_line) + (COLS - R) * pick_side
-    pick = jnp.where(pick_cell == target, 1.0, 0.0).astype(BF16)
-
+    def picker(first, count, cells, first_cell):
+        line = iota((2 * count, cells), 0)
+        side = (line >= count).astype(jnp.int32)
+        strip_cell = line - count * side + first
+        row = jnp.floor((strip_cell.astype(F32) + 0.5) * (1.0 / R)).astype(jnp.int32)
+        wanted = row * COLS + (strip_cell - R * row) + (COLS - R) * side - first_cell
+        return jnp.where(iota((2 * count, cells), 1) == wanted, 1.0, 0.0).astype(BF16)
+
+    pick = picker(0, STRIP, PCELLS, 0)
+
+    land_row = land_vector[...].reshape(1, D)
     lead_index = iota((lead_table.shape[0], 1), 0)
     lead_rows = [
         jnp.sum(
@@ -331,28 +412,46 @@
         for l in (0, 1)
     ]
 
-    def project(l, p):
+    def store_strips(l, picked, start, count, part, lanes):
+        sent = dot(picked, part).astype(BF16)
+        rows = pl.ds(pl.multiple_of(start, 16), count)
+        strips[l, 0, rows, lanes] = sent[:count]
+        strips[l, 1, rows, lanes] = sent[count:]
+
+    def keys_values(l, start, size, done, before_value=lambda: None):
+        rows = pl.ds(pl.multiple_of(start, BCELLS), size)
+        cond = x_buf[l, rows, :].astype(F32) + lead_rows[l] + land[rows, :] * land_row
+        mean_square = jnp.mean(cond * cond, axis=1, keepdims=True)
+        flat = (cond * lax.rsqrt(mean_square + 1e-05) * norm_gain[...]).astype(BF16)
+        normed[rows, :] = flat
+        inner_rows = pl.ds(pl.multiple_of(start + R * COLS, 16), size)
+        for weight, lanes in ((wk, pl.ds(0, INNER)), (wv, pl.ds(INNER, INNER))):
+            if weight is wv:
+                before_value()
+            part = dot(flat, weight[...])
+            part = unit(part) if weight is wk else part.astype(BF16)
+            own[l, inner_rows, lanes] = part
+            done(part, lanes)
+
+    def piece_keys_values(l, p):
         c = piece_at(p)
-        rows = pl.ds(pl.multiple_of(c * PCELLS, PCELLS), PCELLS)
-        cond = (
-            x_buf[l, rows, :].astype(F32) + lead_rows[l] + land[rows, :] * land_vector[...]
-        )
-        mean_square = jnp.mean(cond * cond, axis=1, keepdims=True)
-        normed = (cond * lax.rsqrt(mean_square + 1e-05) * norm_gain[...]).astype(BF16)
-        inner_rows = pl.ds(pl.multiple_of(c * PCELLS + R * COLS, 16), PCELLS)
-        strip_rows = pl.ds(pl.multiple_of(c * STRIP, 16), STRIP)
-
-        def finish(part, lanes):
-            own[l, inner_rows, lanes] = part
-            sent = dot(pick, part).astype(BF16)
-            strips[l, 0, strip_rows, lanes] = sent[:STRIP]
-            strips[l, 1, strip_rows, lanes] = sent[STRIP:]
-
-        finish(unit(dot(normed, wk[...])), pl.ds(0, INNER))
-        finish(dot(normed, wv[...]).astype(BF16), pl.ds(INNER, INNER))
-        for copy in z_copies(l, p):
-            copy.start()
-        query[rows, :] = unit(dot(normed, wq[...]))
+
+        def done(part, lanes):
+            store_strips(l, pick, c * STRIP, STRIP, part, lanes)
+
+        def before_value():
+            if l == 0:
+                pl.when(p == 0)(load_value.wait)
+
+        keys_values(l, c * PCELLS, PCELLS, done, before_value)
+        if l == 0:
+            pl.when(p < PIECES - 1)(lambda: start_z(l, p))
+        else:
+            start_z(l, p)
+
+    def queries(start, size):
+        rows = pl.ds(pl.multiple_of(start, BCELLS), size)
+        query[rows, :] = unit(dot(normed[rows, :], wq[...]))
 
     def attend(l, i):
         b = block_at(i)
@@ -417,97 +516,185 @@
             for h in range(PER_GROUP):
                 part = mixed[h * BCELLS : (h + 1) * BCELLS] * inverses[h]
                 total = jnp.where(lane_head == h, part, total)
-            attended[:, k_lanes] = total.astype(BF16)
-        moved = x_buf[l, rows, :].astype(F32) + dot(attended[...], wo[...])
-        state[rows, :] = moved.astype(BF16)
-
-    def project_loop(l, low, high):
-        def body(p, carry):
-            project(l, p)
-            return carry
-
-        lax.fori_loop(low, high, body, 0)
-
-    for load in loads[:4]:
-        load.wait()
-    project_loop(0, 0, 1)
-    start_edge_own(0, 0)
-    project_loop(0, 1, PIECES)
+            attended[rows, k_lanes] = total.astype(BF16)
+
+    def project_out(l, start, size):
+        rows = pl.ds(pl.multiple_of(start, BCELLS), size)
+        moved = x_buf[l, rows, :].astype(F32) + dot(attended[rows, :], wo[...])
+        (state if l == 0 else final)[rows, :] = moved.astype(BF16)
+
+    def order(i):
+        return lax.rem(i + 2, 4) + 2 * lax.shift_right_logical(i, 2)
+
+    load_key.wait()
+
+    def first_project(p, carry):
+        load_piece(p).wait()
+
+        @pl.when(p == 1)
+        def _():
+            start_edge_own(0, 0)
+            load_query.start()
+            load_out.start()
+
+        piece_keys_values(0, p)
+        return carry
+
+    pl.semaphore_wait(barrier, 3 + has_early.astype(jnp.int32) + has_late.astype(jnp.int32))
+    lax.fori_loop(0, PIECES, first_project, 0)
+    start_z(0, PIECES)
+    start_z(0, PIECES + 1)
     start_edge_own(0, 1)
-    loads[4].wait()
+    for copy in pole_copies:
+        copy.start()
+    load_query.wait()
+
+    def first_query(p, carry):
+        queries(piece_at(p) * PCELLS, PCELLS)
+        return carry
+
+    lax.fori_loop(0, PIECES, first_query, 0)
+    start_corners(0)
+    load_out.wait()
     for copy in pole_copies:
         copy.wait_recv()
     build_flags()
     wait_z(0, 0)
-    start_edge_sides(0, 0)
     wait_z(0, 1)
-    wait_edges(0, 0)
+    wait_z(0, PIECES)
 
     def first_body(i, carry):
+        block = order(i)
+
+        @pl.when(i == 1)
+        def _():
+            wait_z(0, PIECES + 1)
+            start_late_sides(0)
+
         @pl.when(i == 2)
         def _():
-            wait_z(0, 2)
-            start_edge_sides(0, 1)
+            wait_corners(0)
 
         @pl.when(i == 4)
         def _():
-            wait_edges(0, 1)
-
-        attend(0, i)
-        section_copy(i).start()
+            wait_late(0)
+
+        attend(0, block)
+
+        @pl.when(i < 2)
+        def _():
+            project_out(0, block_at(block) * BCELLS, BCELLS)
+            section_copy(block).start()
+
+        @pl.when((i == 3) | (i == 5))
+        def _():
+            project_out(0, piece_at(lax.shift_right_logical(block, 1)) * PCELLS, PCELLS)
+            section_copy(block - 1).start()
+            section_copy(block).start()
+
         return carry
 
     lax.fori_loop(0, BLOCKS, first_body, 0)
 
-    for i in (0, 1):
-        section_copy(i).wait_recv()
-    project_loop(1, 0, 1)
-    start_edge_own(1, 0)
-    for i in (2, 3):
-        section_copy(i).wait_recv()
-    project_loop(1, 1, 2)
+    def second_project(step, carry):
+        p = 1 - step
+        section_copy(2 * p).wait_recv()
+        section_copy(2 * p + 1).wait_recv()
+        piece_keys_values(1, p)
+
+        @pl.when(step == 1)
+        def _():
+            start_edge_own(1, 0)
+
+        queries(piece_at(p) * PCELLS, PCELLS)
+        return carry
+
+    lax.fori_loop(0, PIECES - 1, second_project, 0)
+
+    def last_piece():
+        c = piece_at(PIECES - 1)
+        section_copy(4).wait_recv()
+        block = block_at(4)
+        start, count = part_at(PIECES)
+        half = (block - 2 * c) * BCELLS
+        picked = picker(start - c * STRIP, count, BCELLS, half)
+
+        def done(part, lanes):
+            store_strips(1, picked, start, count, part, lanes)
+
+        keys_values(1, block * BCELLS, BCELLS, done)
+        start_z(1, PIECES)
+        queries(block * BCELLS, BCELLS)
+        start_corners(1)
+
+        section_copy(5).wait_recv()
+        block = block_at(5)
+        start, count = part_at(PIECES + 1)
+        picked = picker(start - c * STRIP, count, PCELLS, 0)
+        keys_values(1, block * BCELLS, BCELLS, lambda part, lanes: None)
+        rows = pl.ds(pl.multiple_of(c * PCELLS + R * COLS, 16), PCELLS)
+        for lanes in (pl.ds(0, INNER), pl.ds(INNER, INNER)):
+            store_strips(1, picked, start, count, own[1, rows, lanes], lanes)
+        start_z(1, PIECES + 1)
+        start_edge_own(1, 1)
+        queries(block * BCELLS, BCELLS)
+
+    half_cells = CELLS // 2
+
+    def second_body(i, carry):
+        block = lax.rem(i + 2, 3) + 3 * lax.div(i, 3)
+        block = jnp.where(i < 3, block, i)
+
+        @pl.when(i == 1)
+        def _():
+            wait_corners(1)
+
+        @pl.when(i == 3)
+        def _():
+            project_out(1, flip * half_cells, half_cells)
+            for j in range(3):
+                out_copy(j).start()
+            wait_z(1, PIECES + 1)
+            start_late_sides(1)
+
+        @pl.when(i == 4)
+        def _():
+            wait_late(1)
+
+        attend(1, block)
+        return carry
+
+    last_piece()
+    wait_z(1, 1)
+    wait_z(1, 0)
+    wait_z(1, PIECES)
+    lax.fori_loop(0, BLOCKS, second_body, 0)
+    project_out(1, (1 - flip) * half_cells, half_cells)
+    for j in range(3, BLOCKS):
+        out_copy(j).start()
+
+    for copy in pole_copies:
+        copy.wait_send()
     for i in range(BLOCKS):
         section_copy(i).wait_send()
-    wait_z(1, 0)
-    start_edge_sides(1, 0)
-    wait_z(1, 1)
-    wait_edges(1, 0)
-
-    def second_body(i, carry):
-        @pl.when(i == 2)
-        def _():
-            for j in (4, 5):
-                section_copy(j).wait_recv()
-            project(1, 2)
-            start_edge_own(1, 1)
-            wait_z(1, 2)
-            start_edge_sides(1, 1)
-
-        @pl.when(i == 4)
-        def _():
-            wait_edges(1, 1)
-
-        attend(1, i)
-        out_copy(i).start()
-        return carry
-
-    lax.fori_loop(0, BLOCKS, second_body, 0)
-
+    for l in (0, 1):
+        for p in (0, 1, PIECES, PIECES + 1):
+            for copy in z_copies(l, p):
+                copy.wait_send()
+
+        def early_sent(l=l):
+            edge_copies(l, 0, (0,))[0].wait_send()
+            for copy in corner_copies(l):
+                copy.wait_send()
+
+        def late_sent(l=l):
+            for copy in edge_copies(l, 1, (0, 1, 2)):
+                copy.wait_send()
+
+        edge_when(0, early_sent)
+        edge_when(1, late_sent)
     for i in range(BLOCKS):
         out_copy(i).wait()
-    for copy in pole_copies:
-        copy.wait_send()
-    for l in (0, 1):
-        for p in range(PIECES):
-            for copy in z_copies(l, p):
-                copy.wait_send()
-        for which in (0, 1):
-
-            def act(l=l, which=which):
-                for copy in edge_copies(l, which, (0, 1, 2)):
-                    copy.wait_send()
-
-            edge_when(which, act)
 
 
 def per_device(
@@ -526,16 +713,22 @@
     w_out,
     logit_scale,
 ):
-    vmem = pl.BlockSpec(memory_space=pltpu.VMEM)
     smem = pl.BlockSpec(memory_space=pltpu.SMEM)
     hbm = pl.BlockSpec(memory_space=pl.ANY)
     result = pl.pallas_call(
         functools.partial(kernel, lat_count, lon_count),
         out_shape=jax.ShapeDtypeStruct((CELLS, D), BF16),
-        in_specs=[smem, smem, hbm, vmem, vmem, vmem, vmem, vmem, hbm, hbm, hbm, hbm],
+        in_specs=[smem, smem] + [hbm] * 10,
         out_specs=hbm,
         scratch_shapes=[
+            pltpu.VMEM((COLS, ROWS), jnp.int32),
+            pltpu.VMEM((COLS, ROWS), jnp.int32),
+            pltpu.VMEM(lead_table.shape, F32),
+            pltpu.VMEM(land_vector.shape, F32),
+            pltpu.VMEM(norm_gain.shape, F32),
             pltpu.VMEM((2, CELLS, D), BF16),
+            pltpu.VMEM((CELLS, D), BF16),
+            pltpu.VMEM((CELLS, D), BF16),
             pltpu.VMEM((CELLS, D), BF16),
             pltpu.VMEM((D, INNER), BF16),
             pltpu.VMEM((D, INNER), BF16),
@@ -550,11 +743,13 @@
             pltpu.VMEM((SIDE, WIDE), BF16),
             pltpu.VMEM((SIDE, WIDE), BF16),
             pltpu.VMEM((CELLS, 1), F32),
-            pltpu.VMEM((BCELLS, INNER), BF16),
+            pltpu.VMEM((CELLS, INNER), BF16),
             pltpu.VMEM((LANES, LANES), BF16),
-            pltpu.VMEM((ROWS, 128), F32),
-            pltpu.VMEM((2, ROWS, 128), F32),
+            pltpu.VMEM((COLS, 128), F32),
+            pltpu.VMEM((2, COLS, 128), F32),
+            pltpu.VMEM((2, 2, STRIP, D), BF16),
             pltpu.SemaphoreType.DMA((5,)),
+            pltpu.SemaphoreType.DMA((PIECES + 4,)),
             pltpu.SemaphoreType.DMA((BLOCKS,)),
             pltpu.SemaphoreType.DMA((2, SLOTS)),
             pltpu.SemaphoreType.DMA((2, SLOTS)),
@@ -570,10 +765,10 @@
         lead_steps,
         logit_scale,
         fields.reshape(CELLS, D),
-        land_sea,
-        pole_valid,
+        land_sea.T,
+        pole_valid.T,
         lead_table,
-        land_vector.reshape(1, D),
+        land_vector,
         norm_gain,
         w_query[0],
         w_key[0],

time: 83.3 us -> 71 us (0.85)
  Pallas kernels: 76.6 us -> 67.7 us
  local copies, waits for them, and re-layouts: 6.38 us -> 2.36 us
    pallas_call x1, Pallas kernels: 76.6 us -> 67.7 us  [per_device(): pl.pallas_call(functools.partial(kernel, lat_count, lon_count), out_shape...]
    unnamed x3 -> x1, local copies, waits for them, and re-layouts: 5.09 us -> 2.36 us
    reshape x1 -> x0, local copies, waits for them, and re-layouts: 1.29 us -> none  [per_device(): land_vector.reshape(1, D)]
where the time goes in v1:
time: 71 us; the launch traced here: 70.1 us
  Pallas kernels  67.7 us (95%)
  local copies, waits for them, and re-layouts  2.36 us (3%)
    pallas_call x1, Pallas kernels, per_device(): pl.pallas_call(functools.partial(kernel, lat_count, lon_count), out_shape...  67.7 us
    unnamed x1, local copies, waits for them, and re-layouts  2.36 us

profile of v1, /device:TPU:6, one launch (start us, length us, event | category | flops | bytes accessed | tf_op | source)
XLA Modules:
  0.0 70.1 jit_solution(2342825654036364268)
XLA Ops:
  0.0 67.7 %shard_map.118 = bf16[384,1536]{1,0:T(8,128)(2,1)} custom-call(s32[1,2]{1,0:T(1,128)} %lead_steps.1, f32[1,12]{1,0:T(1,128)} %logit_scale.1, bf16[384,1536]{1,0:T(8,128)(2,1)} %bitcast.13, s32[16,24]{1,0:T(8,128)} %bitcast.14, s32[16,24]{1,0:T(8,128)} %bitcast.15, f32[40,1536]{1,0:T(8,128)} %lead_table_in.1, f32[1536]{0:T(1024)} %land_vector_in.1, ...), custom_call_target="tpu_custom_call" | custom-call | tf_op jit(solution)/shard_map/pallas_call | solution.py:718
  67.7 2.4 %copy.14 = bf16[1,24,16,1536]{3,2,1,0:T(8,128)(2,1)} copy(bf16[1,24,16,1536]{3,2,1,0:T(8,128)(2,1)} %bitcast.8) | data formatting | bytes 2359296

commit v2 on v1

--- a/solution.py
+++ b/solution.py
@@ -237,6 +237,10 @@
         for copy in z_copies(l, p):
             copy.start()
 
+    def sent_z(l, p):
+        for copy in z_copies(l, p):
+            copy.wait_send()
+
     def edge_copies(l, which, parts):
         upper = flip if which else 1 - flip
         device = {"lat": late if which else early}
@@ -541,12 +545,11 @@
         return carry
 
     pl.semaphore_wait(barrier, 3 + has_early.astype(jnp.int32) + has_late.astype(jnp.int32))
+    for copy in pole_copies:
+        copy.start()
     lax.fori_loop(0, PIECES, first_project, 0)
     start_z(0, PIECES)
-    start_z(0, PIECES + 1)
     start_edge_own(0, 1)
-    for copy in pole_copies:
-        copy.start()
     load_query.wait()
 
     def first_query(p, carry):
@@ -554,6 +557,9 @@
         return carry
 
     lax.fori_loop(0, PIECES, first_query, 0)
+    for p in (0, 1, PIECES):
+        sent_z(0, p)
+    start_z(0, PIECES + 1)
     start_corners(0)
     load_out.wait()
     for copy in pole_copies:
@@ -589,15 +595,19 @@
         @pl.when((i == 3) | (i == 5))
         def _():
             project_out(0, piece_at(lax.shift_right_logical(block, 1)) * PCELLS, PCELLS)
-            section_copy(block - 1).start()
-            section_copy(block).start()
 
         return carry
 
     lax.fori_loop(0, BLOCKS, first_body, 0)
+
+    def send_after(block, earlier):
+        section_copy(earlier).wait_send()
+        section_copy(block).start()
 
     def second_project(step, carry):
         p = 1 - step
+        send_after(4 * step, 2 * p)
+        send_after(4 * step + 1, 2 * p + 1)
         section_copy(2 * p).wait_recv()
         section_copy(2 * p + 1).wait_recv()
         piece_keys_values(1, p)
@@ -675,12 +685,12 @@
 
     for copy in pole_copies:
         copy.wait_send()
-    for i in range(BLOCKS):
+    for i in (4, 5):
         section_copy(i).wait_send()
+    sent_z(0, PIECES + 1)
+    for p in (0, 1, PIECES, PIECES + 1):
+        sent_z(1, p)
     for l in (0, 1):
-        for p in (0, 1, PIECES, PIECES + 1):
-            for copy in z_copies(l, p):
-                copy.wait_send()
 
         def early_sent(l=l):
             edge_copies(l, 0, (0,))[0].wait_send()

time: 71 us -> 68.3 us (0.962)
  Pallas kernels: 67.7 us -> 65 us
    pallas_call x1, Pallas kernels: 67.7 us -> 65 us  [per_device(): pl.pallas_call(functools.partial(kernel, lat_count, lon_count), out_shape...]
where the time goes in v2:
time: 68.3 us; the launch traced here: 67.4 us
  Pallas kernels  65 us (95%)
  local copies, waits for them, and re-layouts  2.36 us (3%)
    pallas_call x1, Pallas kernels, per_device(): pl.pallas_call(functools.partial(kernel, lat_count, lon_count), out_shape...  65 us
    unnamed x1, local copies, waits for them, and re-layouts  2.36 us

profile of v2, /device:TPU:6, one launch (start us, length us, event | category | flops | bytes accessed | tf_op | source)
XLA Modules:
  0.0 67.4 jit_solution(1352415375998162045)
XLA Ops:
  0.0 65.0 %shard_map.118 = bf16[384,1536]{1,0:T(8,128)(2,1)} custom-call(s32[1,2]{1,0:T(1,128)} %lead_steps.1, f32[1,12]{1,0:T(1,128)} %logit_scale.1, bf16[384,1536]{1,0:T(8,128)(2,1)} %bitcast.13, s32[16,24]{1,0:T(8,128)} %bitcast.14, s32[16,24]{1,0:T(8,128)} %bitcast.15, f32[40,1536]{1,0:T(8,128)} %lead_table_in.1, f32[1536]{0:T(1024)} %land_vector_in.1, ...), custom_call_target="tpu_custom_call" | custom-call | tf_op jit(solution)/shard_map/pallas_call | solution.py:728
  65.0 2.4 %copy.14 = bf16[1,24,16,1536]{3,2,1,0:T(8,128)(2,1)} copy(bf16[1,24,16,1536]{3,2,1,0:T(8,128)(2,1)} %bitcast.8) | data formatting | bytes 2359296

commit v3 on v2

--- a/solution.py
+++ b/solution.py
@@ -109,6 +109,7 @@
     pole_mine,
     pole_side,
     corners,
+    biases,
     small_sem,
     load_sem,
     out_sem,
@@ -457,14 +458,15 @@
         rows = pl.ds(pl.multiple_of(start, BCELLS), size)
         query[rows, :] = unit(dot(normed[rows, :], wq[...]))
 
-    def attend(l, i):
-        b = block_at(i)
-        rows = pl.ds(pl.multiple_of(b * BCELLS, BCELLS), BCELLS)
+    def key_rows(b):
         own_rows = pl.ds(pl.multiple_of(b * BCELLS, BCELLS), 16 * COLS)
-        side_rows = pl.ds(
-            pl.multiple_of(16 * lax.shift_right_logical(6 * b + 3, 2), 16), REACH
-        )
-        spare = jnp.zeros((SPARE, LANES), BF16)
+        side = 16 * lax.shift_right_logical(6 * b + 3, 2)
+        return own_rows, pl.ds(pl.multiple_of(side, 16), REACH)
+
+    spare = jnp.zeros((SPARE, LANES), BF16)
+
+    def build_bias(b, carry):
+        own_rows, side_rows = key_rows(b)
         q_cell = iota((BCELLS, WIDE), 0)
         lane = iota((BCELLS, WIDE), 1)
         q_row = lax.shift_right_logical(q_cell, 4) + b * BROWS
@@ -475,7 +477,14 @@
         flags = jnp.concatenate(
             [flag_own[own_rows, :], flag_left[side_rows, :], flag_right[side_rows, :], spare[:, :WIDE]], axis=0
         )
-        bias = jnp.where(dot_t(wanted, flags) > 2.5, 0.0, LOW)
+        biases[b] = jnp.where(dot_t(wanted, flags) > 2.5, 0.0, LOW)
+        return carry
+
+    def attend(l, i):
+        b = block_at(i)
+        rows = pl.ds(pl.multiple_of(b * BCELLS, BCELLS), BCELLS)
+        own_rows, side_rows = key_rows(b)
+        bias = biases[b]
         lane_head = lax.shift_right_logical(iota((1, LANES), 1), 6)
         for g in range(GROUPS):
             k_lanes = pl.ds(g * LANES, LANES)
@@ -528,7 +537,7 @@
         (state if l == 0 else final)[rows, :] = moved.astype(BF16)
 
     def order(i):
-        return lax.rem(i + 2, 4) + 2 * lax.shift_right_logical(i, 2)
+        return jnp.where(i < 3, lax.rem(i + 2, 3), i)
 
     load_key.wait()
 
@@ -565,6 +574,7 @@
     for copy in pole_copies:
         copy.wait_recv()
     build_flags()
+    lax.fori_loop(0, BLOCKS, build_bias, 0)
     wait_z(0, 0)
     wait_z(0, 1)
     wait_z(0, PIECES)
@@ -577,8 +587,6 @@
             wait_z(0, PIECES + 1)
             start_late_sides(0)
 
-        @pl.when(i == 2)
-        def _():
             wait_corners(0)
 
         @pl.when(i == 4)
@@ -587,12 +595,15 @@
 
         attend(0, block)
 
-        @pl.when(i < 2)
+        @pl.when(i < 4)
         def _():
             project_out(0, block_at(block) * BCELLS, BCELLS)
+
+        @pl.when(i < 3)
+        def _():
             section_copy(block).start()
 
-        @pl.when((i == 3) | (i == 5))
+        @pl.when(i == 5)
         def _():
             project_out(0, piece_at(lax.shift_right_logical(block, 1)) * PCELLS, PCELLS)
 
@@ -605,14 +616,22 @@
         section_copy(block).start()
 
     def second_project(step, carry):
-        p = 1 - step
-        send_after(4 * step, 2 * p)
-        send_after(4 * step + 1, 2 * p + 1)
+        p = step
+
+        @pl.when(step == 0)
+        def _():
+            send_after(3, 2)
+            send_after(4, 0)
+
+        @pl.when(step == 1)
+        def _():
+            send_after(5, 1)
+
         section_copy(2 * p).wait_recv()
         section_copy(2 * p + 1).wait_recv()
         piece_keys_values(1, p)
 
-        @pl.when(step == 1)
+        @pl.when(step == 0)
         def _():
             start_edge_own(1, 0)
 
@@ -685,7 +704,7 @@
 
     for copy in pole_copies:
         copy.wait_send()
-    for i in (4, 5):
+    for i in (3, 4, 5):
         section_copy(i).wait_send()
     sent_z(0, PIECES + 1)
     for p in (0, 1, PIECES, PIECES + 1):
@@ -758,6 +777,7 @@
             pltpu.VMEM((COLS, 128), F32),
             pltpu.VMEM((2, COLS, 128), F32),
             pltpu.VMEM((2, 2, STRIP, D), BF16),
+            pltpu.VMEM((BLOCKS, BCELLS, 512), F32),
             pltpu.SemaphoreType.DMA((5,)),
             pltpu.SemaphoreType.DMA((PIECES + 4,)),
             pltpu.SemaphoreType.DMA((BLOCKS,)),

time: 68.3 us -> 65.5 us (0.959)
  Pallas kernels: 65 us -> 62.1 us
    pallas_call x1, Pallas kernels: 65 us -> 62.1 us  [per_device(): pl.pallas_call(functools.partial(kernel, lat_count, lon_count), out_shape...]
where the time goes in v3:
time: 65.5 us; the launch traced here: 64.5 us
  Pallas kernels  62.1 us (95%)
  local copies, waits for them, and re-layouts  2.36 us (4%)
    pallas_call x1, Pallas kernels, per_device(): pl.pallas_call(functools.partial(kernel, lat_count, lon_count), out_shape...  62.1 us
    unnamed x1, local copies, waits for them, and re-layouts  2.36 us

profile of v3, /device:TPU:6, one launch (start us, length us, event | category | flops | bytes accessed | tf_op | source)
XLA Modules:
  0.0 64.5 jit_solution(13536306697994575130)
XLA Ops:
  0.0 62.1 %shard_map.118 = bf16[384,1536]{1,0:T(8,128)(2,1)} custom-call(s32[1,2]{1,0:T(1,128)} %lead_steps.1, f32[1,12]{1,0:T(1,128)} %logit_scale.1, bf16[384,1536]{1,0:T(8,128)(2,1)} %bitcast.13, s32[16,24]{1,0:T(8,128)} %bitcast.14, s32[16,24]{1,0:T(8,128)} %bitcast.15, f32[40,1536]{1,0:T(8,128)} %lead_table_in.1, f32[1536]{0:T(1024)} %land_vector_in.1, ...), custom_call_target="tpu_custom_call" | custom-call | tf_op jit(solution)/shard_map/pallas_call | solution.py:747
  62.1 2.4 %copy.14 = bf16[1,24,16,1536]{3,2,1,0:T(8,128)(2,1)} copy(bf16[1,24,16,1536]{3,2,1,0:T(8,128)(2,1)} %bitcast.8) | data formatting | bytes 2359296

commit v4 on v3

--- a/solution.py
+++ b/solution.py
@@ -566,15 +566,15 @@
         return carry
 
     lax.fori_loop(0, PIECES, first_query, 0)
+    for copy in pole_copies:
+        copy.wait_recv()
+    build_flags()
     for p in (0, 1, PIECES):
         sent_z(0, p)
     start_z(0, PIECES + 1)
     start_corners(0)
+    lax.fori_loop(0, BLOCKS, build_bias, 0)
     load_out.wait()
-    for copy in pole_copies:
-        copy.wait_recv()
-    build_flags()
-    lax.fori_loop(0, BLOCKS, build_bias, 0)
     wait_z(0, 0)
     wait_z(0, 1)
     wait_z(0, PIECES)

time: 65.5 us -> 65.5 us (level)
  no operation moved by 1% of the time
where the time goes in v4:
time: 65.5 us; the launch traced here: 64.5 us
  Pallas kernels  62.1 us (95%)
  local copies, waits for them, and re-layouts  2.36 us (4%)
    pallas_call x1, Pallas kernels, per_device(): pl.pallas_call(functools.partial(kernel, lat_count, lon_count), out_shape...  62.1 us
    unnamed x1, local copies, waits for them, and re-layouts  2.36 us

profile of v4, /device:TPU:6, one launch (start us, length us, event | category | flops | bytes accessed | tf_op | source)
XLA Modules:
  0.0 64.5 jit_solution(17112441217944769758)
XLA Ops:
  0.0 62.1 %shard_map.118 = bf16[384,1536]{1,0:T(8,128)(2,1)} custom-call(s32[1,2]{1,0:T(1,128)} %lead_steps.1, f32[1,12]{1,0:T(1,128)} %logit_scale.1, bf16[384,1536]{1,0:T(8,128)(2,1)} %bitcast.13, s32[16,24]{1,0:T(8,128)} %bitcast.14, s32[16,24]{1,0:T(8,128)} %bitcast.15, f32[40,1536]{1,0:T(8,128)} %lead_table_in.1, f32[1536]{0:T(1024)} %land_vector_in.1, ...), custom_call_target="tpu_custom_call" | custom-call | tf_op jit(solution)/shard_map/pallas_call | solution.py:747
  62.1 2.4 %copy.14 = bf16[1,24,16,1536]{3,2,1,0:T(8,128)(2,1)} copy(bf16[1,24,16,1536]{3,2,1,0:T(8,128)(2,1)} %bitcast.8) | data formatting | bytes 2359296
